TPU v7x, 512 devices: a whole 4x4x16 slice. The times are simulated.
512 devices in a mesh: row: 16 (over z), col: 8 (over x, core), rep: 4 (over y).
Axes of the slice: x: 4, y: 4, z: 16, core: 2. Of those that a mesh axis runs over, the one named last changes fastest.
Arguments:
- density: bfloat16 [6144, 6144], P('row', 'col'), as said below
- keep_square: int32 [48, 48], P('row', 'col'), may hold values 0 or 1
- keep_cube: int32 [48, 48], P('row', 'col'), may hold values 0 or 1
Outputs:
- purified: float32 [6144, 6144], P(('row', 'rep'), 'col')
Inputs may be any that keep to these rules, and one draw needn't show every extreme that they name: density is symmetric; its 128 x 128 diagonal blocks are always occupied, any other block may be zero or occupied at any distance from the diagonal.
All inputs are finite; a program needn't handle non-finite values. No bound on the sum of `keep_square` or of `keep_cube` on one device may be relied on, other than what follows from the above.
Results may differ from a plain program's by a relative error of at most 0.002.
Values may be sent and summed in bfloat16 or wider, within the bound.
No kernel may reach another device: no remote copies, remote signals or barrier semaphores. Data moves between devices by JAX's collectives and lax.ppermute only.
A program may use at most 64 MiB of HBM per device.

v0:
```python
import jax
import jax.numpy as jnp
from jax import lax
from jax.sharding import PartitionSpec as P

BLK = 128
TOP = 16384.0
TINY = 1.1754943508222875e-38
PAD = 16


def encode(piece):
    values = piece.astype(jnp.float32)
    largest = jnp.max(jnp.abs(values), axis=0, keepdims=True)
    exponent = jnp.floor(jnp.log2(jnp.maximum(largest, TINY)))
    coded = (values * jnp.exp2(-exponent) * TOP).astype(jnp.float16)
    header = jnp.broadcast_to(exponent, (PAD, piece.shape[1])).astype(jnp.float16)
    return jnp.concatenate([coded, header], axis=0)


def decode(coded, count):
    parts = coded.reshape(count, -1, coded.shape[1]).astype(jnp.float32)
    height = parts.shape[1] - PAD
    scale = jnp.exp2(parts[:, height : height + 1, :])
    values = (parts[:, :height, :] * (1.0 / TOP) * scale).astype(jnp.bfloat16)
    return values.reshape(count * height, coded.shape[1])


def local(density, keep_square, keep_cube):
    tile_rows, tile_cols = density.shape
    reps = lax.axis_size("rep")
    row_count = lax.axis_size("row")
    col_count = lax.axis_size("col")
    rep = lax.axis_index("rep")
    own = tile_rows // reps
    halves = tile_cols // tile_rows

    def section(array):
        cut = [
            lax.dynamic_slice_in_dim(array, half * tile_rows + rep * own, own, 0)
            for half in range(halves)
        ]
        return jnp.concatenate(cut, axis=0)

    right_piece = lax.dynamic_slice_in_dim(density, rep * own, own, 0)
    left_piece = section(density.T)
    left = decode(lax.all_gather(encode(left_piece), "col", axis=0, tiled=True), col_count)
    right = decode(lax.all_gather(encode(right_piece), "row", axis=0, tiled=True), row_count)

    def contract(a, b):
        return lax.dot_general(a, b, (((0,), (0,)), ((), ())), preferred_element_type=jnp.float32)

    partial = contract(right, left)
    partial = partial.reshape(halves, reps, own, tile_rows).transpose(1, 0, 2, 3)
    partial = partial.reshape(reps, halves * own, tile_rows)
    square_t = jnp.sum(lax.all_to_all(partial, "rep", 0, 0), axis=0)
    mask_rows = section(jnp.repeat(keep_square.T.astype(jnp.float32), BLK, axis=0))
    square_t = square_t * jnp.repeat(mask_rows, BLK, axis=1)
    low = decode(
        lax.all_gather(encode(square_t.astype(jnp.bfloat16)), "col", axis=0, tiled=True), col_count
    )
    cube = contract(low, right)
    mask = jnp.repeat(jnp.repeat(keep_cube.astype(jnp.float32), BLK, axis=0), BLK, axis=1)
    placed = jnp.zeros((tile_cols, tile_rows), jnp.float32)
    for half in range(halves):
        placed = lax.dynamic_update_slice_in_dim(
            placed, square_t[half * own : (half + 1) * own], half * tile_rows + rep * own, 0
        )
    total = 3.0 * placed.T - 2.0 * cube * mask
    pieces = lax.all_to_all(total.reshape(reps, own, tile_cols), "rep", 0, 0)
    return jnp.sum(pieces, axis=0)


def solution(mesh):
    return jax.shard_map(
        local,
        mesh=mesh,
        in_specs=(P("row", "col"), P("row", "col"), P("row", "col")),
        out_specs=P(("row", "rep"), "col"),
        check_vma=False,
    )
```

profile of v0, /device:TPU:1, one launch (start us, length us, event | category | flops | bytes accessed | tf_op | source)
XLA Modules:
  0.0 156.7 jit_solution(12126970050853005048)
XLA Ops:
  0.0 0.9 fusion.11
  1.0 1.0 fusion.13
  2.0 49.8 %all-gather.3 = f16[1792,768]{1,0:T(8,128)(2,1)S(1)} all-gather(f16[112,768]{1,0:T(8,128)(2,1)S(1)} %pad_maximum_fusion.3), channel_id=1, replica_groups=mesh['row'=16,'col'=8,'rep'=4] {'row'}, dimensions={0}, use_global_device_ids=true | all-gather | bytes 2924544 | tf_op jit(solution)/shard_map/all_gather | solution.py:48
  51.8 0.5 convert.3
  52.5 0.5 fusion
  53.0 2.4 %copy.12 = bf16[1536,768]{0,1:T(8,128)(2,1)} copy(bf16[1536,768]{1,0:T(8,128)(2,1)S(1)} %bitcast.59) | data formatting | bytes 4718592 | tf_op jit(solution)/shard_map/reshape | solution.py:26
  55.5 1.1 dynamic-slice_bitcast_fusion.1
  56.6 0.2 fusion.5
  57.3 0.2 copy.13
  57.5 21.3 %all-gather.4 = f16[1664,384]{1,0:T(8,128)(2,1)S(1)} all-gather(f16[208,384]{1,0:T(8,128)(2,1)S(1)} %copy.13), channel_id=1, replica_groups=mesh['row'=16,'col'=8,'rep'=4] {'col'}, dimensions={0}, use_global_device_ids=true | all-gather | bytes 1437696 | tf_op jit(solution)/shard_map/all_gather | solution.py:47
  79.1 0.2 fusion.2
  79.3 1.4 copy-done
  80.7 1.4 convolution_bitcast_fusion
  82.1 1.1 copy.14
  83.3 4.4 %all-to-all-start = ((f32[4,192,384]{2,1,0:T(8,128)}), f32[4,192,384]{2,1,0:T(8,128)}, u32[]{:S(2)}, u32[]{:S(2)}) async-start(f32[4,192,384]{2,1,0:T(8,128)} %bitcast.13), calls=%async_computation | async-start | bytes 2359296 | tf_op jit(solution)/shard_map/all_to_all | solution.py:56
  87.9 1.1 broadcast_in_dim.40
  89.0 1.6 %copy.18 = f32[384,768]{1,0:T(8,128)S(1)} copy(f32[384,768]{0,1:T(8,128)} %bitcast.66) | data formatting | bytes 2359296 | tf_op jit(solution)/shard_map/reshape | solution.py:63
  90.8 13.1 %all-to-all-done = f32[4,192,384]{2,1,0:T(8,128)} async-done(((f32[4,192,384]{2,1,0:T(8,128)}), f32[4,192,384]{2,1,0:T(8,128)}, u32[]{:S(2)}, u32[]{:S(2)}) %all-to-all-start) | async-done | bytes 1179680 | tf_op jit(solution)/shard_map/all_to_all | solution.py:56
  103.9 2.1 %reduce_sum.18 = f32[192,384]{1,0:T(8,128)} reduce(f32[4,192,384]{2,1,0:T(8,128)} %all-to-all-done, f32[]{:T(128)} %constant.15.clone.1), dimensions={0}, to_apply=%region_2.0 | reduce | flops 221184 | bytes 1474564 | tf_op jit(solution)/shard_map/reduce_sum | solution.py:56
  106.0 1.9 %copy.15 = f32[192,384]{0,1:T(8,128)} copy(f32[192,384]{1,0:T(8,128)} %reduce_sum.18) | data formatting | bytes 589824 | tf_op jit(solution)/shard_map/reduce_sum | solution.py:56
  107.9 1.1 fusion.8
  109.0 0.8 fusion.23
  110.1 0.8 pad_maximum_fusion.2
  110.9 1.7 %copy.16 = f16[208,384]{1,0:T(8,128)(2,1)} copy(f16[208,384]{0,1:T(8,128)(2,1)} %pad_maximum_fusion.2) | data formatting | bytes 319488 | tf_op jit(solution)/shard_map/concatenate | solution.py:18
  112.6 15.4 %all-gather.5 = f16[1664,384]{1,0:T(8,128)(2,1)S(1)} all-gather(f16[208,384]{1,0:T(8,128)(2,1)} %copy.16), channel_id=1, replica_groups=mesh['row'=16,'col'=8,'rep'=4] {'col'}, dimensions={0}, use_global_device_ids=true | all-gather | bytes 1437696 | tf_op jit(solution)/shard_map/all_gather | solution.py:60
  128.2 1.2 fusion.1
  129.4 1.1 broadcast_in_dim.16
  130.6 2.0 %dynamic_update_slice.6 = f32[768,384]{0,1:T(8,128)} dynamic-update-slice(f32[768,384]{0,1:T(8,128)} %broadcast_in_dim.16, f32[96,384]{0,1:T(8,128)} %get-tuple-element.10, s32[]{:T(128)S(6)} %select_n.14, s32[]{:T(128)} %constant.18.clone.1) | dynamic-update-slice | bytes 294916 | tf_op jit(solution)/shard_map/dynamic_update_slice | solution.py:66
  132.5 1.9 %dynamic_update_slice.7 = f32[768,384]{0,1:T(8,128)} dynamic-update-slice(f32[768,384]{0,1:T(8,128)} %dynamic_update_slice.6, f32[96,384]{0,1:T(8,128)} %get-tuple-element.9, s32[]{:T(128)S(6)} %select_n.15, s32[]{:T(128)} %constant.18.clone.1) | dynamic-update-slice | bytes 294916 | tf_op jit(solution)/shard_map/dynamic_update_slice | solution.py:66
  134.5 2.8 %fusion.4 = f32[384,768]{1,0:T(8,128)S(1)} fusion(f32[384,768]{1,0:T(8,128)S(1)} %copy.18, bf16[1536,384]{1,0:T(8,128)(2,1)} %bitcast.65, bf16[1536,768]{1,0:T(8,128)(2,1)S(1)} %bitcast.60, f32[768,384]{0,1:T(8,128)} %dynamic_update_slice.7), kind=kOutput, calls=%fused_computation.9 | convolution fusion | flops 907149312 | bytes 7077888 | tf_op jit(solution)/shard_map/dot_general | solution.py:51
  137.3 18.7 %all_to_all.10 = f32[4,96,768]{2,1,0:T(8,128)S(1)} all-to-all(f32[4,96,768]{2,1,0:T(8,128)S(1)} %bitcast.64), channel_id=1, replica_groups=mesh['row'=16,'col'=8,'rep'=4] {'rep'}, dimensions={0} | all-to-all | bytes 2359296 | tf_op jit(solution)/shard_map/all_to_all | solution.py:70
  155.9 0.8 reduce_sum.19
  (32 shorter events, 1.7 us)
Async XLA Ops:
  79.1 1.7 %copy-start = (bf16[1536,768]{0,1:T(8,128)(2,1)S(1)}, bf16[1536,768]{0,1:T(8,128)(2,1)}, u32[]{:S(2)}) copy-start(bf16[1536,768]{0,1:T(8,128)(2,1)} %copy.12) | copy-start | bytes 7077892
  83.2 4.4 %copy-start.1 = (s32[3,6]{1,0:T(4,128)S(1)}, s32[3,6]{1,0:T(4,128)}, u32[]{:S(2)}) copy-start(s32[3,6]{1,0:T(4,128)} %param.4) | copy-start | bytes 220
  83.2 4.5 %copy-start.2 = (s32[3,6]{1,0:T(4,128)S(1)}, s32[3,6]{1,0:T(4,128)}, u32[]{:S(2)}) copy-start(s32[3,6]{1,0:T(4,128)} %param.5) | copy-start | bytes 220
  83.3 20.7 %all-to-all-start = ((f32[4,192,384]{2,1,0:T(8,128)}), f32[4,192,384]{2,1,0:T(8,128)}, u32[]{:S(2)}, u32[]{:S(2)}) async-start(f32[4,192,384]{2,1,0:T(8,128)} %bitcast.13), calls=%async_computation | async-start | bytes 2359296 | tf_op jit(solution)/shard_map/all_to_all | solution.py:56
where the time goes:
time: 157 us
  blocking collectives  105 us (67%)
  local copies, waits for them, and re-layouts  19.1 us (12%)
  waiting for transfers between devices  13.1 us (8%)
  other arithmetic  10.5 us (7%)
  starting transfers between devices  4.39 us (3%)
  matrix products  4.17 us (3%)
    all_gather x1, blocking collectives, local(): lax.all_gather(encode(right_piece), 'row', axis=0, tiled=True)  49.8 us
    all_gather x1, blocking collectives, local(): lax.all_gather(encode(left_piece), 'col', axis=0, tiled=True)  21.3 us
    all_to_all x1, blocking collectives, local(): pieces = lax.all_to_all(total.reshape(reps, own, tile_cols), 'rep', 0, 0)  18.7 us
    all_gather x1, blocking collectives, local(): lax.all_gather(encode(square_t.astype(jnp.bfloat16)), 'col', axis=0, tile...  15.4 us
    all_to_all x1, waiting for transfers between devices, local(): square_t = jnp.sum(lax.all_to_all(partial, 'rep', 0, 0), axis=0)  13.1 us
    all_to_all x1, starting transfers between devices, local(): square_t = jnp.sum(lax.all_to_all(partial, 'rep', 0, 0), axis=0)  4.39 us
    dot_general x2, matrix products, contract(): lax.dot_general(a, b, (((0,), (0,)), ((), ())), preferred_element_type=jn...  4.17 us
    dynamic_update_slice x2, local copies, waits for them, and re-layouts, local(): lax.dynamic_update_slice_in_dim(placed, square_t[half * own:(half + 1) *...  3.9 us
  transfers between devices with their start and end apart: 1, of which 1 were waited for; matrix products, arithmetic and copies ran while one was open for 2% of the time, Pallas kernels for 0%

commit v1 on v0

--- a/solution.py
+++ b/solution.py
@@ -7,6 +7,13 @@
 TOP = 16384.0
 TINY = 1.1754943508222875e-38
 PAD = 16
+
+
+def divide_circles_up(local_values, net_axis):
+    oldest = lax.all_to_all(
+        jnp.concatenate([local_values] * lax.axis_size(net_axis), 0), net_axis, 0, 0, tiled=True
+    )
+    return oldest
 
 
 def encode(piece):
@@ -44,7 +51,7 @@
 
     right_piece = lax.dynamic_slice_in_dim(density, rep * own, own, 0)
     left_piece = section(density.T)
-    left = decode(lax.all_gather(encode(left_piece), "col", axis=0, tiled=True), col_count)
+    left = decode(divide_circles_up(encode(left_piece), "col"), col_count)
     right = decode(lax.all_gather(encode(right_piece), "row", axis=0, tiled=True), row_count)
 
     def contract(a, b):

time: 157 us -> 146 us (0.930)
  blocking collectives: 105 us -> 85.8 us
  starting transfers between devices: 4.39 us -> 15.5 us
  waiting for transfers between devices: 13.1 us -> 7.3 us
  local copies, waits for them, and re-layouts: 19.1 us -> 22.8 us
    all_gather x1 -> x0, blocking collectives: 21.3 us -> none  [local(): lax.all_gather(encode(left_piece), 'col', axis=0, tiled=True)]
    all_to_all x0 -> x1, starting transfers between devices: none -> 11.1 us  [divide_circles_up(): lax.all_to_all(jnp.concatenate([local_values] * lax.axis_size(net_axis),...]
    all_gather x1, blocking collectives: 15.4 us -> 22.5 us  [local(): lax.all_gather(encode(square_t.astype(jnp.bfloat16)), 'col', axis=0, tile...]
    all_to_all x1, waiting for transfers between devices: 13.1 us -> 7.3 us  [local(): square_t = jnp.sum(lax.all_to_all(partial, 'rep', 0, 0), axis=0)]
    all_gather x1, blocking collectives: 49.8 us -> 44.7 us  [local(): lax.all_gather(encode(right_piece), 'row', axis=0, tiled=True)]
    concatenate x0 -> x2, local copies, waits for them, and re-layouts: none -> 3.84 us  [divide_circles_up(): jnp.concatenate([local_values] * lax.axis_size(net_axis), 0)]
  transfers between devices with their start and end apart: 1 -> 2, of which waited for: 1 -> 1; matrix products, arithmetic and copies ran while one was open for 2% -> 5% of each run, Pallas kernels for 0% -> 0%
where the time goes in v1:
time: 146 us
  blocking collectives  85.8 us (59%)
  local copies, waits for them, and re-layouts  22.8 us (16%)
  starting transfers between devices  15.5 us (11%)
  other arithmetic  9.92 us (7%)
  waiting for transfers between devices  7.3 us (5%)
  matrix products  4.18 us (3%)
    all_gather x1, blocking collectives, local(): lax.all_gather(encode(right_piece), 'row', axis=0, tiled=True)  44.7 us
    all_gather x1, blocking collectives, local(): lax.all_gather(encode(square_t.astype(jnp.bfloat16)), 'col', axis=0, tile...  22.5 us
    all_to_all x1, blocking collectives, local(): pieces = lax.all_to_all(total.reshape(reps, own, tile_cols), 'rep', 0, 0)  18.6 us
    all_to_all x1, starting transfers between devices, divide_circles_up(): lax.all_to_all(jnp.concatenate([local_values] * lax.axis_size(net_axis),...  11.1 us
    all_to_all x1, waiting for transfers between devices, local(): square_t = jnp.sum(lax.all_to_all(partial, 'rep', 0, 0), axis=0)  7.3 us
    all_to_all x1, starting transfers between devices, local(): square_t = jnp.sum(lax.all_to_all(partial, 'rep', 0, 0), axis=0)  4.39 us
    dot_general x2, matrix products, contract(): lax.dot_general(a, b, (((0,), (0,)), ((), ())), preferred_element_type=jn...  4.18 us
    dynamic_update_slice x2, local copies, waits for them, and re-layouts, local(): lax.dynamic_update_slice_in_dim(placed, square_t[half * own:(half + 1) *...  3.92 us
  transfers between devices with their start and end apart: 2, of which 1 were waited for; matrix products, arithmetic and copies ran while one was open for 5% of the time, Pallas kernels for 0%

profile of v1, /device:TPU:1, one launch (start us, length us, event | category | flops | bytes accessed | tf_op | source)
XLA Modules:
  0.0 145.7 jit_solution(1225307709783766593)
XLA Ops:
  0.0 1.1 dynamic-slice_bitcast_fusion.1
  1.1 0.2 fusion.5
  1.7 1.9 %concatenate.19 = f16[1664,384]{0,1:T(8,128)(2,1)S(1)} concatenate(f16[192,384]{0,1:T(8,128)(2,1)S(1)} %fusion.7, f16[16,384]{0,1:T(8,128)(2,1)S(1)} %broadcast_in_dim.35, f16[192,384]{0,1:T(8,128)(2,1)S(1)} %fusion.7, f16[16,384]{0,1:T(8,128)(2,1)S(1)} %broadcast_in_dim.35, f16[192,384]{0,1:T(8,128)(2,1)S(1)} %fusion.7, f16[16,384]{0,1:T(8,128)(2,1)S(1)} %broadcast_in_dim.35, ...), dimensions={0} | concatenate | bytes 2555904 | tf_op jit(solution)/shard_map/concatenate | solution.py:14
  3.7 1.9 %copy.13 = f16[1664,384]{1,0:T(8,128)(2,1)} copy(f16[1664,384]{0,1:T(8,128)(2,1)S(1)} %concatenate.19) | data formatting | bytes 2555904 | tf_op jit(solution)/shard_map/concatenate | solution.py:14
  5.6 11.1 %all-to-all-start = ((f16[8,208,384]{2,1,0:T(8,128)(2,1)}), f16[8,208,384]{2,1,0:T(8,128)(2,1)}, u32[]{:S(2)}, u32[]{:S(2)}) async-start(f16[8,208,384]{2,1,0:T(8,128)(2,1)} %bitcast.7), calls=%async_computation | async-start | bytes 2555904 | tf_op jit(solution)/shard_map/all_to_all | solution.py:13
  16.9 44.7 %all-gather.2 = f16[1792,768]{1,0:T(8,128)(2,1)S(1)} all-gather(f16[112,768]{1,0:T(8,128)(2,1)S(1)} %pad_maximum_fusion.2), channel_id=1, replica_groups=mesh['row'=16,'col'=8,'rep'=4] {'row'}, dimensions={0}, use_global_device_ids=true | all-gather | bytes 2924544 | tf_op jit(solution)/shard_map/all_gather | solution.py:55
  61.6 0.5 convert.2
  62.2 0.5 fusion
  62.7 2.5 %copy.12 = bf16[1536,768]{0,1:T(8,128)(2,1)} copy(bf16[1536,768]{1,0:T(8,128)(2,1)S(1)} %bitcast.58) | data formatting | bytes 4718592 | tf_op jit(solution)/shard_map/reshape | solution.py:33
  65.2 1.5 %convert_element_type.83 = f32[8,208,384]{2,1,0:T(8,128)S(1)} convert(f16[8,208,384]{2,1,0:T(8,128)(2,1)} %all-to-all-done) | non-fusion elementwise | flops 638976 | bytes 3833856 | tf_op jit(solution)/shard_map/convert_element_type | solution.py:29
  66.7 0.2 fusion.2
  67.0 1.4 copy-done
  68.4 1.4 convolution_bitcast_fusion
  69.8 1.1 copy.14
  70.9 4.4 %all-to-all-start.1 = ((f32[4,192,384]{2,1,0:T(8,128)}), f32[4,192,384]{2,1,0:T(8,128)}, u32[]{:S(2)}, u32[]{:S(2)}) async-start(f32[4,192,384]{2,1,0:T(8,128)} %bitcast.12), calls=%async_computation.1 | async-start | bytes 2359296 | tf_op jit(solution)/shard_map/all_to_all | solution.py:63
  75.6 1.1 broadcast_in_dim.40
  76.7 1.6 %copy.18 = f32[384,768]{1,0:T(8,128)S(1)} copy(f32[384,768]{0,1:T(8,128)} %bitcast.64) | data formatting | bytes 2359296 | tf_op jit(solution)/shard_map/reshape | solution.py:70
  78.5 7.3 %all-to-all-done.1 = f32[4,192,384]{2,1,0:T(8,128)} async-done(((f32[4,192,384]{2,1,0:T(8,128)}), f32[4,192,384]{2,1,0:T(8,128)}, u32[]{:S(2)}, u32[]{:S(2)}) %all-to-all-start.1) | async-done | bytes 1179680 | tf_op jit(solution)/shard_map/all_to_all | solution.py:63
  85.8 2.1 %reduce_sum.18 = f32[192,384]{1,0:T(8,128)} reduce(f32[4,192,384]{2,1,0:T(8,128)} %all-to-all-done.1, f32[]{:T(128)} %constant.15.clone.1), dimensions={0}, to_apply=%region_2.0 | reduce | flops 221184 | bytes 1474564 | tf_op jit(solution)/shard_map/reduce_sum | solution.py:63
  87.9 1.9 %copy.15 = f32[192,384]{0,1:T(8,128)} copy(f32[192,384]{1,0:T(8,128)} %reduce_sum.18) | data formatting | bytes 589824 | tf_op jit(solution)/shard_map/reduce_sum | solution.py:63
  89.8 1.1 fusion.8
  90.9 0.8 fusion.23
  92.0 0.8 pad_maximum_fusion.1
  92.8 1.7 %copy.16 = f16[208,384]{1,0:T(8,128)(2,1)} copy(f16[208,384]{0,1:T(8,128)(2,1)} %pad_maximum_fusion.1) | data formatting | bytes 319488 | tf_op jit(solution)/shard_map/concatenate | solution.py:25
  94.5 22.5 %all-gather.3 = f16[1664,384]{1,0:T(8,128)(2,1)S(1)} all-gather(f16[208,384]{1,0:T(8,128)(2,1)} %copy.16), channel_id=1, replica_groups=mesh['row'=16,'col'=8,'rep'=4] {'col'}, dimensions={0}, use_global_device_ids=true | all-gather | bytes 1437696 | tf_op jit(solution)/shard_map/all_gather | solution.py:67
  117.2 1.2 fusion.1
  118.4 1.1 broadcast_in_dim.16
  119.6 2.0 %dynamic_update_slice.6 = f32[768,384]{0,1:T(8,128)} dynamic-update-slice(f32[768,384]{0,1:T(8,128)} %broadcast_in_dim.16, f32[96,384]{0,1:T(8,128)} %get-tuple-element.10, s32[]{:T(128)S(6)} %select_n.14, s32[]{:T(128)} %constant.18.clone.1) | dynamic-update-slice | bytes 294916 | tf_op jit(solution)/shard_map/dynamic_update_slice | solution.py:73
  121.5 2.0 %dynamic_update_slice.7 = f32[768,384]{0,1:T(8,128)} dynamic-update-slice(f32[768,384]{0,1:T(8,128)} %dynamic_update_slice.6, f32[96,384]{0,1:T(8,128)} %get-tuple-element.9, s32[]{:T(128)S(6)} %select_n.15, s32[]{:T(128)} %constant.18.clone.1) | dynamic-update-slice | bytes 294916 | tf_op jit(solution)/shard_map/dynamic_update_slice | solution.py:73
  123.5 2.8 %fusion.4 = f32[384,768]{1,0:T(8,128)S(1)} fusion(f32[384,768]{1,0:T(8,128)S(1)} %copy.18, bf16[1536,384]{1,0:T(8,128)(2,1)} %bitcast.63, bf16[1536,768]{1,0:T(8,128)(2,1)S(1)} %bitcast.59, f32[768,384]{0,1:T(8,128)} %dynamic_update_slice.7), kind=kOutput, calls=%fused_computation.9 | convolution fusion | flops 907149312 | bytes 7077888 | tf_op jit(solution)/shard_map/dot_general | solution.py:58
  126.3 18.6 %all_to_all.19 = f32[4,96,768]{2,1,0:T(8,128)S(1)} all-to-all(f32[4,96,768]{2,1,0:T(8,128)S(1)} %bitcast.62), channel_id=1, replica_groups=mesh['row'=16,'col'=8,'rep'=4] {'rep'}, dimensions={0} | all-to-all | bytes 2359296 | tf_op jit(solution)/shard_map/all_to_all | solution.py:77
  144.9 0.8 reduce_sum.19
  (35 shorter events, 1.5 us)
Async XLA Ops:
  5.6 11.2 %copy-start.1 = (bf16[384,768]{1,0:T(8,128)(2,1)S(1)}, bf16[384,768]{1,0:T(8,128)(2,1)}, u32[]{:S(2)}) copy-start(bf16[384,768]{1,0:T(8,128)(2,1)} %param.3) | copy-start | bytes 1769476
  5.6 59.7 %all-to-all-start = ((f16[8,208,384]{2,1,0:T(8,128)(2,1)}), f16[8,208,384]{2,1,0:T(8,128)(2,1)}, u32[]{:S(2)}, u32[]{:S(2)}) async-start(f16[8,208,384]{2,1,0:T(8,128)(2,1)} %bitcast.7), calls=%async_computation | async-start | bytes 2555904 | tf_op jit(solution)/shard_map/all_to_all | solution.py:13
  66.7 1.7 %copy-start = (bf16[1536,768]{0,1:T(8,128)(2,1)S(1)}, bf16[1536,768]{0,1:T(8,128)(2,1)}, u32[]{:S(2)}) copy-start(bf16[1536,768]{0,1:T(8,128)(2,1)} %copy.12) | copy-start | bytes 7077892
  70.9 4.4 %copy-start.2 = (s32[3,6]{1,0:T(4,128)S(1)}, s32[3,6]{1,0:T(4,128)}, u32[]{:S(2)}) copy-start(s32[3,6]{1,0:T(4,128)} %param.4) | copy-start | bytes 220
  70.9 4.5 %copy-start.3 = (s32[3,6]{1,0:T(4,128)S(1)}, s32[3,6]{1,0:T(4,128)}, u32[]{:S(2)}) copy-start(s32[3,6]{1,0:T(4,128)} %param.5) | copy-start | bytes 220
  70.9 14.9 %all-to-all-start.1 = ((f32[4,192,384]{2,1,0:T(8,128)}), f32[4,192,384]{2,1,0:T(8,128)}, u32[]{:S(2)}, u32[]{:S(2)}) async-start(f32[4,192,384]{2,1,0:T(8,128)} %bitcast.12), calls=%async_computation.1 | async-start | bytes 2359296 | tf_op jit(solution)/shard_map/all_to_all | solution.py:63
